TPU v7x, 256 devices: a whole 4x4x8 slice. The times are simulated.
256 devices in a mesh: seq: 32 (over x, z), head: 8 (over y, core).
Axes of the slice: x: 4, y: 4, z: 8, core: 2. Of those that a mesh axis runs over, the one named last changes fastest.
Arguments:
- query_rows: bfloat16 [32768, 5120], P(('seq', 'head')), may hold values from -16 to 16
- key_rows: bfloat16 [32768, 5120], P(('seq', 'head')), may hold values from -16 to 16
- value_rows: bfloat16 [32768, 5120], P(('seq', 'head')), may hold values from -6 to 6
- head_kind: int32 [40], replicated, may hold values from 0 to 1, as said below
- frame_window: int32 [40], replicated, may hold values from 0 to 1, as said below
Outputs:
- attended: bfloat16 [32768, 5120], P(('seq', 'head'))
Inputs may be any that keep to these rules, and one draw needn't show every extreme that they name: `head_kind`: some head is spatial and some head is temporal. `frame_window`: some head has window 1.
All inputs are finite; a program needn't handle non-finite values.
Results may differ from a plain program's by a relative error of at most 0.004.
Values may be sent and summed in bfloat16 or wider, within the bound.
No kernel may reach another device: no remote copies, remote signals or barrier semaphores. Data moves between devices by JAX's collectives and lax.ppermute only.
A program may use at most 64 MiB of HBM per device.

v0:
```python
import functools

import jax
import jax.numpy as jnp
from jax import lax
from jax.experimental import pallas as pl
from jax.experimental.pallas import tpu as pltpu
from jax.sharding import PartitionSpec as P

BF16 = jnp.bfloat16
F32 = jnp.float32
LOG2E = 1.4426950408889634
SMEM = pl.BlockSpec(memory_space=pltpu.SMEM)
HBM = pl.BlockSpec(memory_space=pltpu.HBM)
ANY = pl.BlockSpec(memory_space=pl.ANY)
VMEM = pl.BlockSpec(memory_space=pltpu.VMEM)
MIB = 1024 * 1024
TILE = 16

VARIANTS = (
    (6, 6, 4),
    (10, 10, 10),
)


def in_hbm(value):
    return pltpu.with_memory_space_constraint(value, pltpu.HBM)


def params(vmem=1):
    return pltpu.CompilerParams(vmem_limit_bytes=vmem * MIB)


def cost(flops, bytes_accessed):
    return pl.CostEstimate(flops=flops, bytes_accessed=bytes_accessed, transcendentals=0)


def chip_here():
    return lax.div(lax.axis_index("head"), jnp.int32(2))


def head_loop(kind_ref, win_ref, wide, on_temporal, on_spatial):
    total = kind_ref.shape[0]

    def body(h, counts):
        seen_t, seen_w, seen_n = counts
        is_t = kind_ref[h]
        is_w = (1 - is_t) * win_ref[h]
        is_n = (1 - is_t) * (1 - win_ref[h])
        if on_temporal is not None:
            pl.when(is_t == 1)(lambda: on_temporal(h, seen_t))
        if on_spatial is not None:
            rank = jnp.where(is_w == 1, seen_w, wide + seen_n)
            pl.when(is_t == 0)(lambda: on_spatial(h, rank))
        return seen_t + is_t, seen_w + is_w, seen_n + is_n

    zero = jnp.int32(0)
    return lax.fori_loop(0, total, body, (zero, zero, zero))


def columns(h, width):
    return pl.ds(pl.multiple_of(h * width, width), width)


def wait_for(count, make):
    def body(_, carry):
        make().wait()
        return carry

    lax.fori_loop(0, count, body, 0)


def pack_temporal(kind, win, rows, slots, width):
    chunks = rows[0].shape[0]

    def kernel(kind_ref, win_ref, q_ref, k_ref, v_ref, out_ref, sem):
        def copy(a, ref, h, t):
            quarter = lax.div(t, jnp.int32(slots))
            slot = lax.rem(t, jnp.int32(slots))
            return pltpu.make_async_copy(
                ref.at[:, :, columns(h, width)],
                out_ref.at[pl.ds(quarter * chunks, chunks), a, slot],
                sem,
            )

        def on_temporal(h, t):
            for a, ref in enumerate((q_ref, k_ref, v_ref)):
                copy(a, ref, h, t).start()

        seen, _, _ = head_loop(kind_ref, win_ref, 0, on_temporal, None)
        wait_for(seen * 3, lambda: copy(0, q_ref, jnp.int32(0), jnp.int32(0)))

    return pl.pallas_call(
        kernel,
        out_shape=jax.ShapeDtypeStruct((4 * chunks, 3, slots, TILE, width), BF16),
        in_specs=[SMEM] * 2 + [HBM] * 3,
        out_specs=VMEM,
        scratch_shapes=[pltpu.SemaphoreType.DMA],
        compiler_params=params(8),
        cost_estimate=cost(0, 8 * slots * chunks * 3 * TILE * width * 2),
        name="pack_temporal",
    )(kind, win, *rows)


def pack_spatial(kind, win, w_count, rows, first, slots, width, after=()):
    count = rows[0].shape[0]

    def kernel(kind_ref, win_ref, wide_ref, q_ref, k_ref, v_ref, *rest):
        outs, sem = rest[-5:-1], rest[-1]
        here = chip_here()

        def copy(a, ref, h, slot, out_ref):
            return pltpu.make_async_copy(ref.at[:, columns(h, width)], out_ref.at[slot, a], sem)

        def on_spatial(h, r):
            slot = lax.div(r, jnp.int32(4)) - first
            step = lax.rem(lax.rem(r, jnp.int32(4)) + 4 - here, jnp.int32(4))
            inside = (slot >= 0) & (slot < slots)
            for d in range(4):

                @pl.when(inside & (step == d))
                def _(d=d):
                    for a, ref in enumerate((q_ref, k_ref, v_ref)):
                        copy(a, ref, h, slot, outs[d]).start()

        _, wide, narrow = head_loop(kind_ref, win_ref, wide_ref[0], None, on_spatial)
        held = jnp.clip(wide + narrow - 4 * first, 0, 4 * slots)
        wait_for(held * 3, lambda: copy(0, q_ref, jnp.int32(0), jnp.int32(0), outs[0]))

    return pl.pallas_call(
        kernel,
        out_shape=[jax.ShapeDtypeStruct((slots, 3, count, width), BF16)] * 4,
        in_specs=[SMEM] * 3 + [HBM] * 3 + [ANY] * len(after),
        out_specs=[VMEM] * 4,
        scratch_shapes=[pltpu.SemaphoreType.DMA],
        compiler_params=params(8),
        cost_estimate=cost(0, 4 * slots * 3 * count * width),
        name="pack_spatial",
    )(kind, win, w_count, *rows, *after)


def assemble(blocks, first, slots):
    _, _, rows, width = blocks[0].shape

    def kernel(*refs):
        ins, out, sems = refs[:4], refs[4], refs[5]
        copies = [
            pltpu.make_async_copy(
                ins[d].at[pl.ds(first, slots), pl.ds(1, 2)], out.at[:, :, d], sems.at[d]
            )
            for d in range(4)
        ]
        for c in copies:
            c.start()
        for c in copies:
            c.wait()

    return pl.pallas_call(
        kernel,
        out_shape=jax.ShapeDtypeStruct((slots, 2, 4, rows, width), BF16),
        in_specs=[VMEM] * 4,
        out_specs=VMEM,
        scratch_shapes=[pltpu.SemaphoreType.DMA((4,))],
        compiler_params=params(8),
        cost_estimate=cost(0, 4 * slots * rows * width),
        name="assemble",
    )(*blocks).reshape(slots, 2, 4 * rows, width)


def gate(parts, after):
    count = len(parts)

    def kernel(*refs):
        ins, outs, sems = refs[:count], refs[-count - 1 : -1], refs[-1]
        copies = [pltpu.make_async_copy(ins[i], outs[i], sems.at[i]) for i in range(count)]
        for c in copies:
            c.start()
        for c in copies:
            c.wait()

    return pl.pallas_call(
        kernel,
        out_shape=[jax.ShapeDtypeStruct(p.shape, BF16) for p in parts],
        in_specs=[VMEM] * count + [ANY] * len(after),
        out_specs=[VMEM] * count,
        scratch_shapes=[pltpu.SemaphoreType.DMA((count,))],
        compiler_params=params(16),
        cost_estimate=cost(0, 1024),
        name="gate",
    )(*parts, *after)


def attend(query, pairs, scale, mask=None, counts=None):
    counts = counts or [None] * len(pairs)
    scores = [
        lax.dot_general(query, key, (((1,), (1,)), ((), ())), preferred_element_type=F32)
        for key, _ in pairs
    ]
    if mask is not None:
        scores = [jnp.where(mask, s, F32(-1e30)) for s in scores]
    tops = [jnp.max(s, axis=1, keepdims=True) for s in scores]
    top = functools.reduce(
        jnp.maximum,
        [t if c is None else jnp.where(c, t, F32(-1e30)) for t, c in zip(tops, counts)],
    )
    total = None
    mixed = None
    for s, t, c, (_, value) in zip(scores, tops, counts, pairs):
        weights = jnp.exp2((s - (top if c is None else jnp.maximum(top, t))) * F32(scale * LOG2E))
        part = jnp.sum(weights, axis=1, keepdims=True)
        out = jnp.dot(weights.astype(BF16), value, preferred_element_type=F32)
        if c is not None:
            part, out = jnp.where(c, part, F32(0.0)), jnp.where(c, out, F32(0.0))
        total = part if total is None else total + part
        mixed = out if mixed is None else mixed + out
    return (mixed / total).astype(BF16)


def temporal_attention(packed, after=()):
    frames, _, slots, tile, width = packed.shape
    group = 8
    rows = frames * group
    scale = width ** (-0.5)

    def kernel(in_ref, *rest):
        out_ref = rest[-1]
        place_q = lax.broadcasted_iota(jnp.int32, (rows, rows), 0) & (group - 1)
        place_k = lax.broadcasted_iota(jnp.int32, (rows, rows), 1) & (group - 1)
        mask = place_q == place_k
        def one(j):
            arrays = [in_ref[:, a, j] for a in range(3)]
            outs = []
            for g in range(0, tile, group):
                query, key, value = (x[:, g : g + group].reshape(rows, width) for x in arrays)
                out = attend(query, [(key, value)], scale, mask)
                outs.append(out.reshape(frames, group, width))
            out_ref[:, j] = jnp.concatenate(outs, axis=1)

        if slots < 8:
            for j in range(slots):
                one(j)
        else:
            pl.loop(0, slots)(one)

    return pl.pallas_call(
        kernel,
        out_shape=jax.ShapeDtypeStruct((frames, slots, tile, width), BF16),
        in_specs=[VMEM] + [ANY] * len(after),
        out_specs=VMEM,
        compiler_params=params(24),
        cost_estimate=cost(0, slots * rows * width),
        name="temporal_attention",
    )(packed, *after)


def spatial_attention(t_count, w_count, blocks, first, count, kvs, heads, after=()):
    _, _, rows, width = blocks[0].shape
    keys = kvs[0].shape[2]
    scale = width ** (-0.5)
    far = len(kvs) > 2

    def kernel(t_ref, w_ref, *refs):
        queries, kv_refs, outs = refs[:4], refs[4 : 4 + len(kvs)], refs[-4:]
        frame = lax.axis_index("seq")
        rank = (pl.program_id(0) + first) * 4 + chip_here()
        used = rank < heads - t_ref[0]

        def run(refs, counts):
            pairs = [(r[0, 0], r[0, 1]) for r in refs]
            for d in range(0, 4, 2):
                query = jnp.concatenate([queries[d][0, 0], queries[d + 1][0, 0]], axis=0)
                out = attend(query, pairs, scale, None, counts)
                outs[d][0] = out[:rows]
                outs[d + 1][0] = out[rows:]

        wide = (rank < w_ref[0]) if far else (rank < 0)
        pl.when(used & jnp.logical_not(wide))(lambda: run(kv_refs[:2], None))
        if far:
            past, coming = frame > 0, frame < lax.axis_size("seq") - 1
            counts = [None, None, past, past, coming, coming]
            pl.when(used & wide)(lambda: run(kv_refs, counts))

    return pl.pallas_call(
        kernel,
        grid=(count,),
        out_shape=[jax.ShapeDtypeStruct((count, rows, width), BF16)] * 4,
        in_specs=[SMEM] * 2
        + [pl.BlockSpec((1, 1, rows, width), lambda j: (j + first, 0, 0, 0))] * 4
        + [pl.BlockSpec((1, 2, keys, width), lambda j: (j, 0, 0, 0))] * len(kvs)
        + [ANY] * len(after),
        out_specs=[pl.BlockSpec((1, rows, width), lambda j: (j, 0, 0))] * 4,
        compiler_params=params(20),
        cost_estimate=cost(0, count * rows * width),
        name="spatial_attention",
    )(t_count, w_count, *[in_hbm(x) for x in (*blocks, *kvs)], *after)


def unpack(kind, win, w_count, temporal, wide_outs, narrow_outs, heads):
    frames, t_slots, tile, width = temporal.shape
    chunks = frames // 4
    wide_slots = wide_outs[0].shape[0]
    outs = list(wide_outs) + list(narrow_outs)
    groups = len(outs) // 4

    def kernel(kind_ref, win_ref, wide_ref, t_ref, *rest):
        s_refs, out_ref, sem = rest[: 4 * groups], rest[4 * groups], rest[4 * groups + 1]
        here = chip_here()

        def copy(h, src):
            return pltpu.make_async_copy(src, out_ref.at[:, :, columns(h, width)], sem)

        def on_temporal(h, t):
            quarter = lax.div(t, jnp.int32(t_slots))
            slot = lax.rem(t, jnp.int32(t_slots))
            copy(h, t_ref.at[pl.ds(quarter * chunks, chunks), slot]).start()

        def on_spatial(h, r):
            slot = lax.div(r, jnp.int32(4))
            step = lax.rem(lax.rem(r, jnp.int32(4)) + 4 - here, jnp.int32(4))
            for g in range(groups):
                inside = slot < wide_slots if g == 0 else slot >= wide_slots
                if groups == 1:
                    inside = slot >= 0
                for d in range(4):

                    @pl.when(inside & (step == d))
                    def _(g=g, d=d):
                        copy(h, s_refs[4 * g + d].at[slot - g * wide_slots]).start()

        head_loop(kind_ref, win_ref, wide_ref[0], on_temporal, on_spatial)
        wait_for(heads, lambda: copy(jnp.int32(0), t_ref.at[pl.ds(0, chunks), 0]))

    return pl.pallas_call(
        kernel,
        out_shape=pltpu.HBM((chunks, tile, heads * width), BF16),
        in_specs=[SMEM] * 3 + [VMEM] * (1 + 4 * groups),
        out_specs=HBM,
        scratch_shapes=[pltpu.SemaphoreType.DMA],
        compiler_params=params(8),
        cost_estimate=cost(0, 2 * heads * chunks * tile * width * 2),
        name="unpack",
    )(kind, win, w_count, temporal, *[in_hbm(o.reshape(-1, chunks, tile, width)) for o in outs])


def y_step(value, by):
    size = lax.axis_size("head")
    pairs = [(i, (i + 2 * by) % size) for i in range(size)]
    return lax.ppermute(value, "head", pairs)


def sibling(value):
    size = lax.axis_size("head")
    return lax.ppermute(value, "head", [(i, i ^ 1) for i in range(size)])


def next_frame(value, by):
    size = lax.axis_size("seq")
    pairs = [(i, i + by) for i in range(size) if 0 <= i + by < size]
    return lax.ppermute(value, "seq", pairs)


def variant(t_slots, s_slots, wide, query_rows, key_rows, value_rows, kind, win, t_count, w_count):
    heads = kind.shape[0]
    count, total_width = query_rows.shape
    width = total_width // heads
    frames = lax.axis_size("seq")
    rows = (query_rows, key_rows, value_rows)
    tiled = [r.reshape(count // TILE, TILE, total_width) for r in rows]

    packed = pack_temporal(kind, win, tiled, t_slots, width)
    arrived = lax.all_to_all(
        packed.reshape(frames, -1, width), "seq", split_axis=0, concat_axis=0, tiled=True
    ).reshape(packed.shape)

    def exchanged(mine, by=1):
        return [mine[0]] + [y_step(mine[d], by * d) for d in range(1, 4)]

    blocks = exchanged(pack_spatial(kind, win, w_count, rows, 0, s_slots, width))
    kv = assemble(blocks, 0, wide)
    before, after = next_frame(kv, 1), next_frame(kv, -1)
    kv_other = sibling(kv)
    narrow_back = []
    if s_slots > wide:
        kv_n = assemble(blocks, wide, s_slots - wide)
        kvs = [kv_n, sibling(kv_n)]
        narrow = spatial_attention(
            t_count, w_count, blocks, wide, s_slots - wide, kvs, heads, [kv_other]
        )
        narrow_back = exchanged(narrow, -1)
    mixed = temporal_attention(arrived, narrow_back[1:])
    before_copy, after_copy = gate([before, after], [mixed])
    kvs = [kv, kv_other, before, sibling(before_copy), after, sibling(after_copy)]
    wide_outs = spatial_attention(t_count, w_count, blocks, 0, wide, kvs, heads, [mixed])
    wide_back = exchanged(wide_outs, -1)
    returned = lax.all_to_all(
        mixed.reshape(frames, -1, width), "seq", split_axis=0, concat_axis=0, tiled=True
    ).reshape(mixed.shape)
    out = unpack(kind, win, w_count, returned, wide_back, narrow_back, heads)
    return out.reshape(count, total_width)


def on_device(query_rows, key_rows, value_rows, head_kind, frame_window):
    heads = head_kind.shape[0]
    t_count = jnp.sum(head_kind)
    w_count = jnp.sum((1 - head_kind) * frame_window)
    t_need = (t_count + 3) // 4
    s_need = (heads - t_count + 3) // 4
    w_need = (w_count + 3) // 4
    choice = jnp.int32(len(VARIANTS) - 1)
    for i in reversed(range(len(VARIANTS) - 1)):
        t_room, s_room, w_room = VARIANTS[i]
        fits = (t_need <= t_room) & (s_need <= s_room) & (w_need <= w_room)
        choice = jnp.where(fits, jnp.int32(i), choice)
    return lax.switch(
        choice,
        [functools.partial(variant, *v) for v in VARIANTS],
        query_rows,
        key_rows,
        value_rows,
        head_kind,
        frame_window,
        t_count.reshape(1),
        w_count.reshape(1),
    )


def solution(mesh):
    split = P(("seq", "head"), None)
    return jax.shard_map(
        on_device,
        mesh=mesh,
        in_specs=(split, split, split, P(), P()),
        out_specs=split,
        check_vma=False,
    )
```

profile of v0, /device:TPU:38, one launch (start us, length us, event | category | flops | bytes accessed | tf_op | source)
XLA Modules:
  0.0 135.6 jit_solution(3341385840798453122)
XLA Ops:
  0.0 1.3 multiply_reduce_fusion
  3.1 132.3 %conditional.1 = (bf16[128,5120]{1,0:T(8,128)(2,1)}) conditional(s32[]{:T(128)} %clamp.3, (bf16[128,5120]{1,0:T(8,128)(2,1)}, bf16[128,5120]{1,0:T(8,128)(2,1)}, bf16[128,5120]{1,0:T(8,128)(2,1)}, s32[40]{0:T(128)}, s32[40]{0:T(128)}, /*index=5*/s32[]{:T(128)}, s32[]{:T(128)}) %tuple.11, (bf16[128,5120]{1,0:T(8,128)(2,1)}, ...), branch_computations={%region_2.3_spmd, %region_3.4_spmd} | conditional | bytes 155159648 | solution.py:414
  3.1 4.1 %pack_temporal.2 = bf16[32,3,6,16,128]{4,3,2,1,0:T(8,128)(2,1)} custom-call(s32[40]{0:T(128)} %get-tuple-element.36.kind_ref, s32[40]{0:T(128)} %get-tuple-element.37.win_ref, bf16[8,16,5120]{2,1,0:T(8,128)(2,1)} %bitcast.49, bf16[8,16,5120]{2,1,0:T(8,128)(2,1)} %bitcast.51, bf16[8,16,5120]{2,1,0:T(8,128)(2,1)} %bitcast.53), custom_call_target="tpu_custom_call" | custom-call | bytes 4718592 | tf_op jit(solution)/shard_map/cond/branch_0_fun/pack_temporal/pallas_call | solution.py:93
  7.3 11.3 %all-to-all-start = ((bf16[32,288,128]{2,1,0:T(8,128)(2,1)}), bf16[32,288,128]{2,1,0:T(8,128)(2,1)}, u32[]{:S(2)}, u32[]{:S(2)}) async-start(bf16[32,288,128]{2,1,0:T(8,128)(2,1)} %bitcast.4), calls=%async_computation | async-start | bytes 4718592 | tf_op jit(solution)/shard_map/cond/branch_0_fun/all_to_all | solution.py:371
  18.7 3.3 %pack_spatial.2 = (bf16[6,3,128,128]{3,2,1,0:T(8,128)(2,1)S(1)}, bf16[6,3,128,128]{3,2,1,0:T(8,128)(2,1)S(1)}, bf16[6,3,128,128]{3,2,1,0:T(8,128)(2,1)S(1)}, bf16[6,3,128,128]{3,2,1,0:T(8,128)(2,1)S(1)}) custom-call(s32[40]{0:T(128)S(1)} %copy-done.33, s32[40]{0:T(128)S(1)} %copy-done.31, s32[1]{0:T(128)} %bitcast.wide_ref.w_ref, ...), custom_call_target="tpu_custom_call" | custom-call | bytes 1179648 | tf_op jit(solution)/shard_map/cond/branch_0_fun/pack_spatial/pallas_call | solution.py:130
  22.0 1.6 %collective-permute-start = (bf16[6,3,128,128]{3,2,1,0:T(8,128)(2,1)S(1)}, bf16[6,3,128,128]{3,2,1,0:T(8,128)(2,1)S(1)}, u32[]{:S(2)}, u32[]{:S(2)}) collective-permute-start(bf16[6,3,128,128]{3,2,1,0:T(8,128)(2,1)S(1)} %get-tuple-element.44), channel_id=1, source_target_pairs={{0,2},{1,3},{2,4},{3,5},{4,6},{5,7},{6,0},{7,1},{8,10},{9,11},{10,... | collective-permute-start | bytes 1769480 | tf_op jit(solution)/shard_map/cond/branch_0_fun/ppermute | solution.py:348
  23.7 2.9 %collective-permute-start.1 = (bf16[6,3,128,128]{3,2,1,0:T(8,128)(2,1)S(1)}, bf16[6,3,128,128]{3,2,1,0:T(8,128)(2,1)S(1)}, u32[]{:S(2)}, u32[]{:S(2)}) collective-permute-start(bf16[6,3,128,128]{3,2,1,0:T(8,128)(2,1)S(1)} %get-tuple-element.45), channel_id=1, source_target_pairs={{0,4},{1,5},{2,6},{3,7},{4,0},{5,1},{6,2},{7,3},{8,12},{9,13},{10,... | collective-permute-start | bytes 1769480 | tf_op jit(solution)/shard_map/cond/branch_0_fun/ppermute | solution.py:348
  26.6 1.4 collective-permute-start.2
  27.9 10.5 %collective-permute-done.refs_1_ = bf16[6,3,128,128]{3,2,1,0:T(8,128)(2,1)S(1)} collective-permute-done((bf16[6,3,128,128]{3,2,1,0:T(8,128)(2,1)S(1)}, bf16[6,3,128,128]{3,2,1,0:T(8,128)(2,1)S(1)}, u32[]{:S(2)}, u32[]{:S(2)}) %collective-permute-start) | collective-permute-done | bytes 589856 | tf_op jit(solution)/shard_map/cond/branch_0_fun/ppermute | solution.py:348
  38.5 13.2 %collective-permute-done.1.refs_2_ = bf16[6,3,128,128]{3,2,1,0:T(8,128)(2,1)S(1)} collective-permute-done((bf16[6,3,128,128]{3,2,1,0:T(8,128)(2,1)S(1)}, bf16[6,3,128,128]{3,2,1,0:T(8,128)(2,1)S(1)}, u32[]{:S(2)}, u32[]{:S(2)}) %collective-permute-start.1) | collective-permute-done | bytes 589856 | tf_op jit(solution)/shard_map/cond/branch_0_fun/ppermute | solution.py:348
  51.7 1.2 assemble.4
  53.0 3.4 %collective-permute-start.8 = (bf16[4,2,512,128]{3,2,1,0:T(8,128)(2,1)}, bf16[4,2,512,128]{3,2,1,0:T(8,128)(2,1)}, u32[]{:S(2)}, u32[]{:S(2)}) collective-permute-start(bf16[4,2,512,128]{3,2,1,0:T(8,128)(2,1)} %bitcast.8.refs_4_), channel_id=1, source_target_pairs={{0,8},{8,16},{16,24},{24,32},{32,40},{40,48},{48,56},{56,64},{64,7... | collective-permute-start | bytes 3145736 | tf_op jit(solution)/shard_map/cond/branch_0_fun/ppermute | solution.py:359
  56.4 2.5 %collective-permute-start.9 = (bf16[4,2,512,128]{3,2,1,0:T(8,128)(2,1)}, bf16[4,2,512,128]{3,2,1,0:T(8,128)(2,1)}, u32[]{:S(2)}, u32[]{:S(2)}) collective-permute-start(bf16[4,2,512,128]{3,2,1,0:T(8,128)(2,1)} %bitcast.8.refs_4_), channel_id=1, source_target_pairs={{8,0},{16,8},{24,16},{32,24},{40,32},{48,40},{56,48},{64,56},{72,6... | collective-permute-start | bytes 3145736 | tf_op jit(solution)/shard_map/cond/branch_0_fun/ppermute | solution.py:359
  59.2 1.9 %collective-permute-done.3.refs_5_ = bf16[2,2,512,128]{3,2,1,0:T(8,128)(2,1)S(1)} collective-permute-done((bf16[2,2,512,128]{3,2,1,0:T(8,128)(2,1)S(1)}, bf16[2,2,512,128]{3,2,1,0:T(8,128)(2,1)S(1)}, u32[]{:S(2)}, u32[]{:S(2)}) %collective-permute-start.3) | collective-permute-done | bytes 524320 | tf_op jit(solution)/shard_map/cond/branch_0_fun/ppermute | solution.py:353
  61.9 3.5 %spatial_attention.3 = (bf16[2,128,128]{2,1,0:T(8,128)(2,1)S(1)}, bf16[2,128,128]{2,1,0:T(8,128)(2,1)S(1)}, bf16[2,128,128]{2,1,0:T(8,128)(2,1)S(1)}, bf16[2,128,128]{2,1,0:T(8,128)(2,1)S(1)}) custom-call(s32[1]{0:T(128)} %bitcast.6.t_ref, s32[1]{0:T(128)} %bitcast.wide_ref.w_ref, bf16[6,3,128,128]{3,2,1,0:T(8,128)(2,1)} %copy-done.2, ...), custom_call_target="tpu_custom_call" | custom-call | bytes 32768 | tf_op jit(solution)/shard_map/cond/branch_0_fun/spatial_attention/pallas_call | solution.py:283
  66.0 1.3 collective-permute-start.5
  67.3 1.0 collective-permute-start.6
  69.0 1.8 %collective-permute-done.5.rest_0_ = bf16[2,128,128]{2,1,0:T(8,128)(2,1)S(1)} collective-permute-done((bf16[2,128,128]{2,1,0:T(8,128)(2,1)S(1)}, bf16[2,128,128]{2,1,0:T(8,128)(2,1)S(1)}, u32[]{:S(2)}, u32[]{:S(2)}) %collective-permute-start.5) | collective-permute-done | bytes 65568 | tf_op jit(solution)/shard_map/cond/branch_0_fun/ppermute | solution.py:348
  70.9 2.8 %collective-permute-done.6.rest_1_ = bf16[2,128,128]{2,1,0:T(8,128)(2,1)S(1)} collective-permute-done((bf16[2,128,128]{2,1,0:T(8,128)(2,1)S(1)}, bf16[2,128,128]{2,1,0:T(8,128)(2,1)S(1)}, u32[]{:S(2)}, u32[]{:S(2)}) %collective-permute-start.6) | collective-permute-done | bytes 65568 | tf_op jit(solution)/shard_map/cond/branch_0_fun/ppermute | solution.py:348
  74.2 4.1 %temporal_attention.2.refs_2_.refs_10_ = bf16[32,6,16,128]{3,2,1,0:T(8,128)(2,1)} custom-call(bf16[32,3,6,16,128]{4,3,2,1,0:T(8,128)(2,1)} %bitcast.5.in_ref, bf16[2,128,128]{2,1,0:T(8,128)(2,1)S(1)} %collective-permute-done.5.rest_0_, bf16[2,128,128]{2,1,0:T(8,128)(2,1)S(1)} %collective-permute-done.6.rest_1_, ...), custom_call_target="tpu_custom_call" | custom-call | bytes 196608 | tf_op jit(solution)/shard_map/cond/branch_0_fun/temporal_attention/pallas_call | solution.py:245
  78.3 11.0 %all-to-all-start.1 = ((bf16[32,96,128]{2,1,0:T(8,128)(2,1)}), bf16[32,96,128]{2,1,0:T(8,128)(2,1)S(1)}, u32[]{:S(2)}, u32[]{:S(2)}) async-start(bf16[32,96,128]{2,1,0:T(8,128)(2,1)} %bitcast.9), calls=%async_computation.1 | async-start | bytes 1572864 | tf_op jit(solution)/shard_map/cond/branch_0_fun/all_to_all | solution.py:395
  89.3 8.8 %collective-permute-done.8.refs_0_.refs_6_ = bf16[4,2,512,128]{3,2,1,0:T(8,128)(2,1)} collective-permute-done((bf16[4,2,512,128]{3,2,1,0:T(8,128)(2,1)}, bf16[4,2,512,128]{3,2,1,0:T(8,128)(2,1)}, u32[]{:S(2)}, u32[]{:S(2)}) %collective-permute-start.8) | collective-permute-done | bytes 1048608 | tf_op jit(solution)/shard_map/cond/branch_0_fun/ppermute | solution.py:359
  98.1 1.7 %gate.2 = (bf16[4,2,512,128]{3,2,1,0:T(8,128)(2,1)S(1)}, bf16[4,2,512,128]{3,2,1,0:T(8,128)(2,1)S(1)}) custom-call(bf16[4,2,512,128]{3,2,1,0:T(8,128)(2,1)} %collective-permute-done.8.refs_0_.refs_6_, bf16[4,2,512,128]{3,2,1,0:T(8,128)(2,1)} %collective-permute-done.9.refs_1_.refs_8_, bf16[32,6,16,128]{3,2,1,0:T(8,128)(2,1)} %temporal_attention.2.refs_2_.refs_10_), custom_call_target="tpu_custom_call" | custom-call | bytes 1024 | tf_op jit(solution)/shard_map/cond/branch_0_fun/gate/pallas_call | solution.py:181
  100.4 2.1 %collective-permute-done.10.refs_7_ = bf16[4,2,512,128]{3,2,1,0:T(8,128)(2,1)S(1)} collective-permute-done((bf16[4,2,512,128]{3,2,1,0:T(8,128)(2,1)S(1)}, bf16[4,2,512,128]{3,2,1,0:T(8,128)(2,1)S(1)}, u32[]{:S(2)}, u32[]{:S(2)}) %collective-permute-start.10) | collective-permute-done | bytes 1048608 | tf_op jit(solution)/shard_map/cond/branch_0_fun/ppermute | solution.py:353
  102.6 1.5 %collective-permute-done.11.refs_9_ = bf16[4,2,512,128]{3,2,1,0:T(8,128)(2,1)S(1)} collective-permute-done((bf16[4,2,512,128]{3,2,1,0:T(8,128)(2,1)S(1)}, bf16[4,2,512,128]{3,2,1,0:T(8,128)(2,1)S(1)}, u32[]{:S(2)}, u32[]{:S(2)}) %collective-permute-start.11) | collective-permute-done | bytes 1048608 | tf_op jit(solution)/shard_map/cond/branch_0_fun/ppermute | solution.py:353
  105.1 11.8 %spatial_attention.4 = (bf16[4,128,128]{2,1,0:T(8,128)(2,1)S(1)}, bf16[4,128,128]{2,1,0:T(8,128)(2,1)S(1)}, bf16[4,128,128]{2,1,0:T(8,128)(2,1)S(1)}, bf16[4,128,128]{2,1,0:T(8,128)(2,1)S(1)}) custom-call(s32[1]{0:T(128)} %bitcast.6.t_ref, s32[1]{0:T(128)} %bitcast.wide_ref.w_ref, bf16[6,3,128,128]{3,2,1,0:T(8,128)(2,1)} %copy-done.2, ...), custom_call_target="tpu_custom_call" | custom-call | bytes 65536 | tf_op jit(solution)/shard_map/cond/branch_0_fun/spatial_attention/pallas_call | solution.py:283
  117.5 3.4 %collective-permute-start.12 = (bf16[4,128,128]{2,1,0:T(8,128)(2,1)S(1)}, bf16[4,128,128]{2,1,0:T(8,128)(2,1)S(1)}, u32[]{:S(2)}, u32[]{:S(2)}) collective-permute-start(bf16[4,128,128]{2,1,0:T(8,128)(2,1)S(1)} %get-tuple-element.53), channel_id=1, source_target_pairs={{0,6},{1,7},{2,0},{3,1},{4,2},{5,3},{6,4},{7,5},{8,14},{9,15},{10,... | collective-permute-start | bytes 393224 | tf_op jit(solution)/shard_map/cond/branch_0_fun/ppermute | solution.py:348
  120.9 1.9 %collective-permute-start.13 = (bf16[4,128,128]{2,1,0:T(8,128)(2,1)S(1)}, bf16[4,128,128]{2,1,0:T(8,128)(2,1)S(1)}, u32[]{:S(2)}, u32[]{:S(2)}) collective-permute-start(bf16[4,128,128]{2,1,0:T(8,128)(2,1)S(1)} %get-tuple-element.54), channel_id=1, source_target_pairs={{0,4},{1,5},{2,6},{3,7},{4,0},{5,1},{6,2},{7,3},{8,12},{9,13},{10,... | collective-permute-start | bytes 393224 | tf_op jit(solution)/shard_map/cond/branch_0_fun/ppermute | solution.py:348
  122.8 3.9 %collective-permute-done.12 = bf16[4,128,128]{2,1,0:T(8,128)(2,1)S(1)} collective-permute-done((bf16[4,128,128]{2,1,0:T(8,128)(2,1)S(1)}, bf16[4,128,128]{2,1,0:T(8,128)(2,1)S(1)}, u32[]{:S(2)}, u32[]{:S(2)}) %collective-permute-start.12) | collective-permute-done | bytes 131104 | tf_op jit(solution)/shard_map/cond/branch_0_fun/ppermute | solution.py:348
  126.8 2.0 %collective-permute-done.13 = bf16[4,128,128]{2,1,0:T(8,128)(2,1)S(1)} collective-permute-done((bf16[4,128,128]{2,1,0:T(8,128)(2,1)S(1)}, bf16[4,128,128]{2,1,0:T(8,128)(2,1)S(1)}, u32[]{:S(2)}, u32[]{:S(2)}) %collective-permute-start.13) | collective-permute-done | bytes 131104 | tf_op jit(solution)/shard_map/cond/branch_0_fun/ppermute | solution.py:348
  128.8 1.7 %collective-permute-done.14 = bf16[4,128,128]{2,1,0:T(8,128)(2,1)S(1)} collective-permute-done((bf16[4,128,128]{2,1,0:T(8,128)(2,1)S(1)}, bf16[4,128,128]{2,1,0:T(8,128)(2,1)S(1)}, u32[]{:S(2)}, u32[]{:S(2)}) %collective-permute-start.14) | collective-permute-done | bytes 131104 | tf_op jit(solution)/shard_map/cond/branch_0_fun/ppermute | solution.py:348
  131.1 4.1 %unpack.2 = bf16[8,16,5120]{2,1,0:T(8,128)(2,1)} custom-call(s32[40]{0:T(128)S(1)} %copy-done.33, s32[40]{0:T(128)S(1)} %copy-done.31, s32[1]{0:T(128)} %bitcast.wide_ref.w_ref, bf16[32,6,16,128]{3,2,1,0:T(8,128)(2,1)S(1)} %bitcast.40, bf16[4,8,16,128]{3,2,1,0:T(8,128)(2,1)} %bitcast.47, bf16[4,8,16,128]{3,2,1,0:T(8,128)(2,1)} %bitcast.60, ...), custom_call_target="tpu_custom_call" | custom-call | bytes 2621440 | tf_op jit(solution)/shard_map/cond/branch_0_fun/unpack/pallas_call | solution.py:333
  (55 shorter events, 5.8 us)
Async XLA Ops:
  7.2 11.4 %copy-start.18 = (bf16[128,5120]{1,0:T(8,128)(2,1)S(1)}, bf16[128,5120]{1,0:T(8,128)(2,1)}, u32[]{:S(2)}) copy-start(bf16[128,5120]{1,0:T(8,128)(2,1)} %get-tuple-element.85.q_ref) | copy-start | bytes 3932164 | tf_op jit(solution)/shard_map/cond
  7.2 11.4 %copy-start.20 = (bf16[128,5120]{1,0:T(8,128)(2,1)S(1)}, bf16[128,5120]{1,0:T(8,128)(2,1)}, u32[]{:S(2)}) copy-start(bf16[128,5120]{1,0:T(8,128)(2,1)} %get-tuple-element.87.k_ref) | copy-start | bytes 3932164 | tf_op jit(solution)/shard_map/cond
  7.2 11.4 %copy-start.31 = (s32[40]{0:T(128)S(1)}, s32[40]{0:T(128)}, u32[]{:S(2)}) copy-start(s32[40]{0:T(128)} %get-tuple-element.37.win_ref) | copy-start | bytes 484 | tf_op jit(solution)/shard_map/cond
  7.3 11.4 %copy-start.33 = (s32[40]{0:T(128)S(1)}, s32[40]{0:T(128)}, u32[]{:S(2)}) copy-start(s32[40]{0:T(128)} %get-tuple-element.36.kind_ref) | copy-start | bytes 484 | tf_op jit(solution)/shard_map/cond
  7.3 66.9 %all-to-all-start = ((bf16[32,288,128]{2,1,0:T(8,128)(2,1)}), bf16[32,288,128]{2,1,0:T(8,128)(2,1)}, u32[]{:S(2)}, u32[]{:S(2)}) async-start(bf16[32,288,128]{2,1,0:T(8,128)(2,1)} %bitcast.4), calls=%async_computation | async-start | bytes 4718592 | tf_op jit(solution)/shard_map/cond/branch_0_fun/all_to_all | solution.py:371
  22.0 37.1 %copy-start.2 = (bf16[6,3,128,128]{3,2,1,0:T(8,128)(2,1)}, bf16[6,3,128,128]{3,2,1,0:T(8,128)(2,1)S(1)}, u32[]{:S(2)}) copy-start(bf16[6,3,128,128]{3,2,1,0:T(8,128)(2,1)S(1)} %get-tuple-element.43.refs_0_) | copy-start | bytes 1769476 | tf_op jit(solution)/shard_map/cond
  22.0 16.4 %collective-permute-start = (bf16[6,3,128,128]{3,2,1,0:T(8,128)(2,1)S(1)}, bf16[6,3,128,128]{3,2,1,0:T(8,128)(2,1)S(1)}, u32[]{:S(2)}, u32[]{:S(2)}) collective-permute-start(bf16[6,3,128,128]{3,2,1,0:T(8,128)(2,1)S(1)} %get-tuple-element.44), channel_id=1, source_target_pairs={{0,2},{1,3},{2,4},{3,5},{4,6},{5,7},{6,0},{7,1},{8,10},{9,11},{10,... | collective-permute-start | bytes 1769480 | tf_op jit(solution)/shard_map/cond/branch_0_fun/ppermute | solution.py:348
  23.7 28.0 %collective-permute-start.1 = (bf16[6,3,128,128]{3,2,1,0:T(8,128)(2,1)S(1)}, bf16[6,3,128,128]{3,2,1,0:T(8,128)(2,1)S(1)}, u32[]{:S(2)}, u32[]{:S(2)}) collective-permute-start(bf16[6,3,128,128]{3,2,1,0:T(8,128)(2,1)S(1)} %get-tuple-element.45), channel_id=1, source_target_pairs={{0,4},{1,5},{2,6},{3,7},{4,0},{5,1},{6,2},{7,3},{8,12},{9,13},{10,... | collective-permute-start | bytes 1769480 | tf_op jit(solution)/shard_map/cond/branch_0_fun/ppermute | solution.py:348
  26.6 25.1 %collective-permute-start.2 = (bf16[6,3,128,128]{3,2,1,0:T(8,128)(2,1)S(1)}, bf16[6,3,128,128]{3,2,1,0:T(8,128)(2,1)S(1)}, u32[]{:S(2)}, u32[]{:S(2)}) collective-permute-start(bf16[6,3,128,128]{3,2,1,0:T(8,128)(2,1)S(1)} %get-tuple-element.46), channel_id=1, source_target_pairs={{0,6},{1,7},{2,0},{3,1},{4,2},{5,3},{6,4},{7,5},{8,14},{9,15},{10,... | collective-permute-start | bytes 1769480 | tf_op jit(solution)/shard_map/cond/branch_0_fun/ppermute | solution.py:348
  38.5 20.6 %copy-start.3 = (bf16[6,3,128,128]{3,2,1,0:T(8,128)(2,1)}, bf16[6,3,128,128]{3,2,1,0:T(8,128)(2,1)S(1)}, u32[]{:S(2)}) copy-start(bf16[6,3,128,128]{3,2,1,0:T(8,128)(2,1)S(1)} %collective-permute-done.refs_1_) | copy-start | bytes 1769476 | tf_op jit(solution)/shard_map/cond
  51.7 7.4 %copy-start.4 = (bf16[6,3,128,128]{3,2,1,0:T(8,128)(2,1)}, bf16[6,3,128,128]{3,2,1,0:T(8,128)(2,1)S(1)}, u32[]{:S(2)}) copy-start(bf16[6,3,128,128]{3,2,1,0:T(8,128)(2,1)S(1)} %collective-permute-done.1.refs_2_) | copy-start | bytes 1769476 | tf_op jit(solution)/shard_map/cond
  51.7 7.4 %copy-start.5 = (bf16[6,3,128,128]{3,2,1,0:T(8,128)(2,1)}, bf16[6,3,128,128]{3,2,1,0:T(8,128)(2,1)S(1)}, u32[]{:S(2)}) copy-start(bf16[6,3,128,128]{3,2,1,0:T(8,128)(2,1)S(1)} %collective-permute-done.2.refs_3_) | copy-start | bytes 1769476 | tf_op jit(solution)/shard_map/cond
  52.9 8.2 %collective-permute-start.4 = (bf16[4,2,512,128]{3,2,1,0:T(8,128)(2,1)}, bf16[4,2,512,128]{3,2,1,0:T(8,128)(2,1)S(1)}, u32[]{:S(2)}, u32[]{:S(2)}) collective-permute-start(bf16[4,2,512,128]{3,2,1,0:T(8,128)(2,1)} %bitcast.8.refs_4_), channel_id=1, source_target_pairs={{0,1},{1,0},{2,3},{3,2},{4,5},{5,4},{6,7},{7,6},{8,9},{9,8},{10,11... | collective-permute-start | bytes 3145736 | tf_op jit(solution)/shard_map/cond/branch_0_fun/ppermute | solution.py:353
  53.0 45.1 %collective-permute-start.8 = (bf16[4,2,512,128]{3,2,1,0:T(8,128)(2,1)}, bf16[4,2,512,128]{3,2,1,0:T(8,128)(2,1)}, u32[]{:S(2)}, u32[]{:S(2)}) collective-permute-start(bf16[4,2,512,128]{3,2,1,0:T(8,128)(2,1)} %bitcast.8.refs_4_), channel_id=1, source_target_pairs={{0,8},{8,16},{16,24},{24,32},{32,40},{40,48},{48,56},{56,64},{64,7... | collective-permute-start | bytes 3145736 | tf_op jit(solution)/shard_map/cond/branch_0_fun/ppermute | solution.py:359
  56.4 41.7 %collective-permute-start.9 = (bf16[4,2,512,128]{3,2,1,0:T(8,128)(2,1)}, bf16[4,2,512,128]{3,2,1,0:T(8,128)(2,1)}, u32[]{:S(2)}, u32[]{:S(2)}) collective-permute-start(bf16[4,2,512,128]{3,2,1,0:T(8,128)(2,1)} %bitcast.8.refs_4_), channel_id=1, source_target_pairs={{8,0},{16,8},{24,16},{32,24},{40,32},{48,40},{56,48},{64,56},{72,6... | collective-permute-start | bytes 3145736 | tf_op jit(solution)/shard_map/cond/branch_0_fun/ppermute | solution.py:359
  59.1 2.0 %copy-start.11 = (bf16[2,2,4,128,128]{4,3,2,1,0:T(8,128)(2,1)}, bf16[2,2,4,128,128]{4,3,2,1,0:T(8,128)(2,1)S(1)}, u32[]{:S(2)}) copy-start(bf16[2,2,4,128,128]{4,3,2,1,0:T(8,128)(2,1)S(1)} %assemble.3) | copy-start | bytes 1572868 | tf_op jit(solution)/shard_map/cond
  59.1 2.0 %collective-permute-start.3 = (bf16[2,2,512,128]{3,2,1,0:T(8,128)(2,1)S(1)}, bf16[2,2,512,128]{3,2,1,0:T(8,128)(2,1)S(1)}, u32[]{:S(2)}, u32[]{:S(2)}) collective-permute-start(bf16[2,2,512,128]{3,2,1,0:T(8,128)(2,1)S(1)} %bitcast.41), channel_id=1, source_target_pairs={{0,1},{1,0},{2,3},{3,2},{4,5},{5,4},{6,7},{7,6},{8,9},{9,8},{10,11... | collective-permute-start | bytes 1572872 | tf_op jit(solution)/shard_map/cond/branch_0_fun/ppermute | solution.py:353
  61.1 17.2 %copy-start.6 = (bf16[4,2,512,128]{3,2,1,0:T(8,128)(2,1)}, bf16[4,2,512,128]{3,2,1,0:T(8,128)(2,1)S(1)}, u32[]{:S(2)}) copy-start(bf16[4,2,512,128]{3,2,1,0:T(8,128)(2,1)S(1)} %collective-permute-done.4.refs_6_.refs_5_) | copy-start | bytes 3145732 | tf_op jit(solution)/shard_map/cond
  66.0 4.9 %collective-permute-start.5 = (bf16[2,128,128]{2,1,0:T(8,128)(2,1)S(1)}, bf16[2,128,128]{2,1,0:T(8,128)(2,1)S(1)}, u32[]{:S(2)}, u32[]{:S(2)}) collective-permute-start(bf16[2,128,128]{2,1,0:T(8,128)(2,1)S(1)} %get-tuple-element.47), channel_id=1, source_target_pairs={{0,6},{1,7},{2,0},{3,1},{4,2},{5,3},{6,4},{7,5},{8,14},{9,15},{10,... | collective-permute-start | bytes 196616 | tf_op jit(solution)/shard_map/cond/branch_0_fun/ppermute | solution.py:348
  67.3 6.4 %collective-permute-start.6 = (bf16[2,128,128]{2,1,0:T(8,128)(2,1)S(1)}, bf16[2,128,128]{2,1,0:T(8,128)(2,1)S(1)}, u32[]{:S(2)}, u32[]{:S(2)}) collective-permute-start(bf16[2,128,128]{2,1,0:T(8,128)(2,1)S(1)} %get-tuple-element.48), channel_id=1, source_target_pairs={{0,4},{1,5},{2,6},{3,7},{4,0},{5,1},{6,2},{7,3},{8,12},{9,13},{10,... | collective-permute-start | bytes 196616 | tf_op jit(solution)/shard_map/cond/branch_0_fun/ppermute | solution.py:348
  68.3 5.8 %collective-permute-start.7 = (bf16[2,128,128]{2,1,0:T(8,128)(2,1)S(1)}, bf16[2,128,128]{2,1,0:T(8,128)(2,1)S(1)}, u32[]{:S(2)}, u32[]{:S(2)}) collective-permute-start(bf16[2,128,128]{2,1,0:T(8,128)(2,1)S(1)} %get-tuple-element.49), channel_id=1, source_target_pairs={{0,2},{1,3},{2,4},{3,5},{4,6},{5,7},{6,0},{7,1},{8,10},{9,11},{10,... | collective-permute-start | bytes 196616 | tf_op jit(solution)/shard_map/cond/branch_0_fun/ppermute | solution.py:348
  70.9 29.0 %copy-start.13 = (bf16[2,128,128]{2,1,0:T(8,128)(2,1)}, bf16[2,128,128]{2,1,0:T(8,128)(2,1)S(1)}, u32[]{:S(2)}) copy-start(bf16[2,128,128]{2,1,0:T(8,128)(2,1)S(1)} %collective-permute-done.5.rest_0_) | copy-start | bytes 196612 | tf_op jit(solution)/shard_map/cond
  73.7 26.1 %copy-start.14 = (bf16[2,128,128]{2,1,0:T(8,128)(2,1)}, bf16[2,128,128]{2,1,0:T(8,128)(2,1)S(1)}, u32[]{:S(2)}) copy-start(bf16[2,128,128]{2,1,0:T(8,128)(2,1)S(1)} %collective-permute-done.6.rest_1_) | copy-start | bytes 196612 | tf_op jit(solution)/shard_map/cond
  74.2 25.7 %copy-start.15 = (bf16[2,128,128]{2,1,0:T(8,128)(2,1)}, bf16[2,128,128]{2,1,0:T(8,128)(2,1)S(1)}, u32[]{:S(2)}) copy-start(bf16[2,128,128]{2,1,0:T(8,128)(2,1)S(1)} %collective-permute-done.7.rest_2_) | copy-start | bytes 196612 | tf_op jit(solution)/shard_map/cond
  78.3 52.2 %all-to-all-start.1 = ((bf16[32,96,128]{2,1,0:T(8,128)(2,1)}), bf16[32,96,128]{2,1,0:T(8,128)(2,1)S(1)}, u32[]{:S(2)}, u32[]{:S(2)}) async-start(bf16[32,96,128]{2,1,0:T(8,128)(2,1)} %bitcast.9), calls=%async_computation.1 | async-start | bytes 1572864 | tf_op jit(solution)/shard_map/cond/branch_0_fun/all_to_all | solution.py:395
  99.8 2.7 %collective-permute-start.10 = (bf16[4,2,512,128]{3,2,1,0:T(8,128)(2,1)S(1)}, bf16[4,2,512,128]{3,2,1,0:T(8,128)(2,1)S(1)}, u32[]{:S(2)}, u32[]{:S(2)}) collective-permute-start(bf16[4,2,512,128]{3,2,1,0:T(8,128)(2,1)S(1)} %get-tuple-element.50), channel_id=1, source_target_pairs={{0,1},{1,0},{2,3},{3,2},{4,5},{5,4},{6,7},{7,6},{8,9},{9,8},{10,11... | collective-permute-start | bytes 3145736 | tf_op jit(solution)/shard_map/cond/branch_0_fun/ppermute | solution.py:353
  99.9 4.1 %collective-permute-start.11 = (bf16[4,2,512,128]{3,2,1,0:T(8,128)(2,1)S(1)}, bf16[4,2,512,128]{3,2,1,0:T(8,128)(2,1)S(1)}, u32[]{:S(2)}, u32[]{:S(2)}) collective-permute-start(bf16[4,2,512,128]{3,2,1,0:T(8,128)(2,1)S(1)} %get-tuple-element.51), channel_id=1, source_target_pairs={{0,1},{1,0},{2,3},{3,2},{4,5},{5,4},{6,7},{7,6},{8,9},{9,8},{10,11... | collective-permute-start | bytes 3145736 | tf_op jit(solution)/shard_map/cond/branch_0_fun/ppermute | solution.py:353
  117.5 9.3 %collective-permute-start.12 = (bf16[4,128,128]{2,1,0:T(8,128)(2,1)S(1)}, bf16[4,128,128]{2,1,0:T(8,128)(2,1)S(1)}, u32[]{:S(2)}, u32[]{:S(2)}) collective-permute-start(bf16[4,128,128]{2,1,0:T(8,128)(2,1)S(1)} %get-tuple-element.53), channel_id=1, source_target_pairs={{0,6},{1,7},{2,0},{3,1},{4,2},{5,3},{6,4},{7,5},{8,14},{9,15},{10,... | collective-permute-start | bytes 393224 | tf_op jit(solution)/shard_map/cond/branch_0_fun/ppermute | solution.py:348
  120.9 7.9 %collective-permute-start.13 = (bf16[4,128,128]{2,1,0:T(8,128)(2,1)S(1)}, bf16[4,128,128]{2,1,0:T(8,128)(2,1)S(1)}, u32[]{:S(2)}, u32[]{:S(2)}) collective-permute-start(bf16[4,128,128]{2,1,0:T(8,128)(2,1)S(1)} %get-tuple-element.54), channel_id=1, source_target_pairs={{0,4},{1,5},{2,6},{3,7},{4,0},{5,1},{6,2},{7,3},{8,12},{9,13},{10,... | collective-permute-start | bytes 393224 | tf_op jit(solution)/shard_map/cond/branch_0_fun/ppermute | solution.py:348
  122.8 7.6 %collective-permute-start.14 = (bf16[4,128,128]{2,1,0:T(8,128)(2,1)S(1)}, bf16[4,128,128]{2,1,0:T(8,128)(2,1)S(1)}, u32[]{:S(2)}, u32[]{:S(2)}) collective-permute-start(bf16[4,128,128]{2,1,0:T(8,128)(2,1)S(1)} %get-tuple-element.55), channel_id=1, source_target_pairs={{0,2},{1,3},{2,4},{3,5},{4,6},{5,7},{6,0},{7,1},{8,10},{9,11},{10,... | collective-permute-start | bytes 393224 | tf_op jit(solution)/shard_map/cond/branch_0_fun/ppermute | solution.py:348
  126.8 3.7 %copy-start.28 = (bf16[4,128,128]{2,1,0:T(8,128)(2,1)}, bf16[4,128,128]{2,1,0:T(8,128)(2,1)S(1)}, u32[]{:S(2)}) copy-start(bf16[4,128,128]{2,1,0:T(8,128)(2,1)S(1)} %collective-permute-done.12) | copy-start | bytes 393220 | tf_op jit(solution)/shard_map/cond
  128.8 1.7 %copy-start.29 = (bf16[4,128,128]{2,1,0:T(8,128)(2,1)}, bf16[4,128,128]{2,1,0:T(8,128)(2,1)S(1)}, u32[]{:S(2)}) copy-start(bf16[4,128,128]{2,1,0:T(8,128)(2,1)S(1)} %collective-permute-done.13) | copy-start | bytes 393220 | tf_op jit(solution)/shard_map/cond
  (6 other events, 5.2 us)
where the time goes:
time: 137 us; the launch traced here: 136 us
  waiting for transfers between devices  50.9 us (37%)
  starting transfers between devices  43.2 us (32%)
  Pallas kernels  34 us (25%)
  local copies, waits for them, and re-layouts  3.71 us (3%)
  between operations  1.99 us (1%)
    ppermute x9, waiting for transfers between devices, y_step(): return lax.ppermute(value, 'head', pairs)  36.5 us
    pallas_call x2, Pallas kernels, spatial_attention(): pl.pallas_call(kernel, grid=(count,), out_shape=[jax.ShapeDtypeStruct((co...  15.3 us
    ppermute x9, starting transfers between devices, y_step(): return lax.ppermute(value, 'head', pairs)  14.3 us
    all_to_all x1, starting transfers between devices, variant(): lax.all_to_all(packed.reshape(frames, -1, width), 'seq', split_axis=0, co...  11.3 us
    all_to_all x1, starting transfers between devices, variant(): lax.all_to_all(mixed.reshape(frames, -1, width), 'seq', split_axis=0, con...  11 us
    ppermute x2, waiting for transfers between devices, next_frame(): return lax.ppermute(value, 'seq', pairs)  8.83 us
    ppermute x2, starting transfers between devices, next_frame(): return lax.ppermute(value, 'seq', pairs)  5.85 us
    ppermute x4, waiting for transfers between devices, sibling(): return lax.ppermute(value, 'head', [(i, i ^ 1) for i in range(size)])  5.55 us
  transfers between devices with their start and end apart: 17, of which 12 were waited for; matrix products, arithmetic and copies ran while one was open for 0% of the time, Pallas kernels for 19%

commit v1 on v0

--- a/solution.py
+++ b/solution.py
@@ -171,20 +171,15 @@
     count = len(parts)
 
     def kernel(*refs):
-        ins, outs, sems = refs[:count], refs[-count - 1 : -1], refs[-1]
-        copies = [pltpu.make_async_copy(ins[i], outs[i], sems.at[i]) for i in range(count)]
-        for c in copies:
-            c.start()
-        for c in copies:
-            c.wait()
+        del refs
 
     return pl.pallas_call(
         kernel,
         out_shape=[jax.ShapeDtypeStruct(p.shape, BF16) for p in parts],
-        in_specs=[VMEM] * count + [ANY] * len(after),
-        out_specs=[VMEM] * count,
-        scratch_shapes=[pltpu.SemaphoreType.DMA((count,))],
-        compiler_params=params(16),
+        in_specs=[ANY] * (count + len(after)),
+        out_specs=[ANY] * count,
+        input_output_aliases={i: i for i in range(count)},
+        compiler_params=params(),
         cost_estimate=cost(0, 1024),
         name="gate",
     )(*parts, *after)
@@ -292,7 +287,7 @@
         compiler_params=params(20),
         cost_estimate=cost(0, count * rows * width),
         name="spatial_attention",
-    )(t_count, w_count, *[in_hbm(x) for x in (*blocks, *kvs)], *after)
+    )(t_count, w_count, *[in_hbm(x) for x in (*blocks, *kvs[:2])], *kvs[2:], *after)
 
 
 def unpack(kind, win, w_count, temporal, wide_outs, narrow_outs, heads):
@@ -388,8 +383,8 @@
         )
         narrow_back = exchanged(narrow, -1)
     mixed = temporal_attention(arrived, narrow_back[1:])
-    before_copy, after_copy = gate([before, after], [mixed])
-    kvs = [kv, kv_other, before, sibling(before_copy), after, sibling(after_copy)]
+    before, after = gate([before, after], [mixed])
+    kvs = [kv, kv_other, before, sibling(before), after, sibling(after)]
     wide_outs = spatial_attention(t_count, w_count, blocks, 0, wide, kvs, heads, [mixed])
     wide_back = exchanged(wide_outs, -1)
     returned = lax.all_to_all(

time: 137 us -> 133 us (0.971)
  waiting for transfers between devices: 50.9 us -> 46.8 us
  starting transfers between devices: 43.2 us -> 46.3 us
  Pallas kernels: 34 us -> 31.9 us
    ppermute x2, waiting for transfers between devices: 8.83 us -> 5.49 us  [next_frame(): return lax.ppermute(value, 'seq', pairs)]
    ppermute x9, starting transfers between devices: 14.3 us -> 17.3 us  [y_step(): return lax.ppermute(value, 'head', pairs)]
    pallas_call x1, Pallas kernels: 1.7 us -> 0.01 us  [gate(): pl.pallas_call(kernel, out_shape=[jax.ShapeDtypeStruct(p.shape, BF16) for...]
    cond x42 -> x38, local copies, waits for them, and re-layouts: 3.71 us -> 2.72 us
  transfers between devices with their start and end apart: 17 -> 17, of which waited for: 12 -> 12; matrix products, arithmetic and copies ran while one was open for 0% -> 0% of each run, Pallas kernels for 19% -> 18%
where the time goes in v1:
time: 133 us; the launch traced here: 132 us
  waiting for transfers between devices  46.8 us (35%)
  starting transfers between devices  46.3 us (35%)
  Pallas kernels  31.9 us (24%)
  local copies, waits for them, and re-layouts  2.72 us (2%)
  between operations  2.18 us (2%)
  other arithmetic  1.38 us (1%)
    ppermute x9, waiting for transfers between devices, y_step(): return lax.ppermute(value, 'head', pairs)  35.5 us
    ppermute x9, starting transfers between devices, y_step(): return lax.ppermute(value, 'head', pairs)  17.3 us
    pallas_call x2, Pallas kernels, spatial_attention(): pl.pallas_call(kernel, grid=(count,), out_shape=[jax.ShapeDtypeStruct((co...  14.8 us
    all_to_all x1, starting transfers between devices, variant(): lax.all_to_all(packed.reshape(frames, -1, width), 'seq', split_axis=0, co...  11.3 us
    all_to_all x1, starting transfers between devices, variant(): lax.all_to_all(mixed.reshape(frames, -1, width), 'seq', split_axis=0, con...  11 us
    ppermute x2, starting transfers between devices, next_frame(): return lax.ppermute(value, 'seq', pairs)  5.85 us
    ppermute x4, waiting for transfers between devices, sibling(): return lax.ppermute(value, 'head', [(i, i ^ 1) for i in range(size)])  5.76 us
    ppermute x2, waiting for transfers between devices, next_frame(): return lax.ppermute(value, 'seq', pairs)  5.49 us
  transfers between devices with their start and end apart: 17, of which 12 were waited for; matrix products, arithmetic and copies ran while one was open for 0% of the time, Pallas kernels for 18%

profile of v1, /device:TPU:38, one launch (start us, length us, event | category | flops | bytes accessed | tf_op | source)
XLA Modules:
  0.0 131.8 jit_solution(13093956589623193420)
XLA Ops:
  0.0 1.4 %multiply_reduce_fusion = (s32[]{:T(128)}, s32[]{:T(128)}) fusion(s32[40]{0:T(128)} %param.11, s32[40]{0:T(128)} %param.10), kind=kLoop, calls=%fused_computation | loop fusion | flops 158 | bytes 328 | tf_op jit(solution)/shard_map/reduce_sum | solution.py:400
  3.4 128.2 %conditional.1 = (bf16[128,5120]{1,0:T(8,128)(2,1)}) conditional(s32[]{:T(128)} %clamp.3, (bf16[128,5120]{1,0:T(8,128)(2,1)}, bf16[128,5120]{1,0:T(8,128)(2,1)}, bf16[128,5120]{1,0:T(8,128)(2,1)}, s32[40]{0:T(128)}, s32[40]{0:T(128)}, /*index=5*/s32[]{:T(128)}, s32[]{:T(128)}) %tuple.11, (bf16[128,5120]{1,0:T(8,128)(2,1)}, ...), branch_computations={%region_2.3_spmd, %region_3.4_spmd} | conditional | bytes 155159648 | solution.py:409
  3.4 4.1 %pack_temporal.2 = bf16[32,3,6,16,128]{4,3,2,1,0:T(8,128)(2,1)} custom-call(s32[40]{0:T(128)} %get-tuple-element.36.kind_ref, s32[40]{0:T(128)} %get-tuple-element.37.win_ref, bf16[8,16,5120]{2,1,0:T(8,128)(2,1)} %bitcast.49, bf16[8,16,5120]{2,1,0:T(8,128)(2,1)} %bitcast.51, bf16[8,16,5120]{2,1,0:T(8,128)(2,1)} %bitcast.53), custom_call_target="tpu_custom_call" | custom-call | bytes 4718592 | tf_op jit(solution)/shard_map/cond/branch_0_fun/pack_temporal/pallas_call | solution.py:93
  7.5 11.3 %all-to-all-start = ((bf16[32,288,128]{2,1,0:T(8,128)(2,1)}), bf16[32,288,128]{2,1,0:T(8,128)(2,1)}, u32[]{:S(2)}, u32[]{:S(2)}) async-start(bf16[32,288,128]{2,1,0:T(8,128)(2,1)} %bitcast.4), calls=%async_computation | async-start | bytes 4718592 | tf_op jit(solution)/shard_map/cond/branch_0_fun/all_to_all | solution.py:366
  18.9 3.5 %pack_spatial.2 = (bf16[6,3,128,128]{3,2,1,0:T(8,128)(2,1)S(1)}, bf16[6,3,128,128]{3,2,1,0:T(8,128)(2,1)S(1)}, bf16[6,3,128,128]{3,2,1,0:T(8,128)(2,1)S(1)}, bf16[6,3,128,128]{3,2,1,0:T(8,128)(2,1)S(1)}) custom-call(s32[40]{0:T(128)S(1)} %copy-done.31, s32[40]{0:T(128)S(1)} %copy-done.29, s32[1]{0:T(128)} %bitcast.wide_ref.w_ref, ...), custom_call_target="tpu_custom_call" | custom-call | bytes 1179648 | tf_op jit(solution)/shard_map/cond/branch_0_fun/pack_spatial/pallas_call | solution.py:130
  22.4 1.6 %collective-permute-start = (bf16[6,3,128,128]{3,2,1,0:T(8,128)(2,1)S(1)}, bf16[6,3,128,128]{3,2,1,0:T(8,128)(2,1)S(1)}, u32[]{:S(2)}, u32[]{:S(2)}) collective-permute-start(bf16[6,3,128,128]{3,2,1,0:T(8,128)(2,1)S(1)} %get-tuple-element.44), channel_id=1, source_target_pairs={{0,2},{1,3},{2,4},{3,5},{4,6},{5,7},{6,0},{7,1},{8,10},{9,11},{10,... | collective-permute-start | bytes 1769480 | tf_op jit(solution)/shard_map/cond/branch_0_fun/ppermute | solution.py:343
  24.1 2.9 %collective-permute-start.1 = (bf16[6,3,128,128]{3,2,1,0:T(8,128)(2,1)S(1)}, bf16[6,3,128,128]{3,2,1,0:T(8,128)(2,1)S(1)}, u32[]{:S(2)}, u32[]{:S(2)}) collective-permute-start(bf16[6,3,128,128]{3,2,1,0:T(8,128)(2,1)S(1)} %get-tuple-element.45), channel_id=1, source_target_pairs={{0,4},{1,5},{2,6},{3,7},{4,0},{5,1},{6,2},{7,3},{8,12},{9,13},{10,... | collective-permute-start | bytes 1769480 | tf_op jit(solution)/shard_map/cond/branch_0_fun/ppermute | solution.py:343
  26.9 1.4 %collective-permute-start.2 = (bf16[6,3,128,128]{3,2,1,0:T(8,128)(2,1)S(1)}, bf16[6,3,128,128]{3,2,1,0:T(8,128)(2,1)S(1)}, u32[]{:S(2)}, u32[]{:S(2)}) collective-permute-start(bf16[6,3,128,128]{3,2,1,0:T(8,128)(2,1)S(1)} %get-tuple-element.46), channel_id=1, source_target_pairs={{0,6},{1,7},{2,0},{3,1},{4,2},{5,3},{6,4},{7,5},{8,14},{9,15},{10,... | collective-permute-start | bytes 1769480 | tf_op jit(solution)/shard_map/cond/branch_0_fun/ppermute | solution.py:343
  28.3 10.5 %collective-permute-done.refs_1_ = bf16[6,3,128,128]{3,2,1,0:T(8,128)(2,1)S(1)} collective-permute-done((bf16[6,3,128,128]{3,2,1,0:T(8,128)(2,1)S(1)}, bf16[6,3,128,128]{3,2,1,0:T(8,128)(2,1)S(1)}, u32[]{:S(2)}, u32[]{:S(2)}) %collective-permute-start) | collective-permute-done | bytes 589856 | tf_op jit(solution)/shard_map/cond/branch_0_fun/ppermute | solution.py:343
  38.8 13.2 %collective-permute-done.1.refs_2_ = bf16[6,3,128,128]{3,2,1,0:T(8,128)(2,1)S(1)} collective-permute-done((bf16[6,3,128,128]{3,2,1,0:T(8,128)(2,1)S(1)}, bf16[6,3,128,128]{3,2,1,0:T(8,128)(2,1)S(1)}, u32[]{:S(2)}, u32[]{:S(2)}) %collective-permute-start.1) | collective-permute-done | bytes 589856 | tf_op jit(solution)/shard_map/cond/branch_0_fun/ppermute | solution.py:343
  52.1 1.2 assemble.4
  53.3 3.4 %collective-permute-start.8 = (bf16[4,2,512,128]{3,2,1,0:T(8,128)(2,1)}, bf16[4,2,512,128]{3,2,1,0:T(8,128)(2,1)}, u32[]{:S(2)}, u32[]{:S(2)}) collective-permute-start(bf16[4,2,512,128]{3,2,1,0:T(8,128)(2,1)} %bitcast.8.refs_4_), channel_id=1, source_target_pairs={{0,8},{8,16},{16,24},{24,32},{32,40},{40,48},{48,56},{56,64},{64,7... | collective-permute-start | bytes 3145736 | tf_op jit(solution)/shard_map/cond/branch_0_fun/ppermute | solution.py:354
  56.7 2.5 %collective-permute-start.9 = (bf16[4,2,512,128]{3,2,1,0:T(8,128)(2,1)}, bf16[4,2,512,128]{3,2,1,0:T(8,128)(2,1)}, u32[]{:S(2)}, u32[]{:S(2)}) collective-permute-start(bf16[4,2,512,128]{3,2,1,0:T(8,128)(2,1)} %bitcast.8.refs_4_), channel_id=1, source_target_pairs={{8,0},{16,8},{24,16},{32,24},{40,32},{48,40},{56,48},{64,56},{72,6... | collective-permute-start | bytes 3145736 | tf_op jit(solution)/shard_map/cond/branch_0_fun/ppermute | solution.py:354
  59.6 1.9 %collective-permute-done.3.refs_5_ = bf16[2,2,512,128]{3,2,1,0:T(8,128)(2,1)S(1)} collective-permute-done((bf16[2,2,512,128]{3,2,1,0:T(8,128)(2,1)S(1)}, bf16[2,2,512,128]{3,2,1,0:T(8,128)(2,1)S(1)}, u32[]{:S(2)}, u32[]{:S(2)}) %collective-permute-start.3) | collective-permute-done | bytes 524320 | tf_op jit(solution)/shard_map/cond/branch_0_fun/ppermute | solution.py:348
  62.2 4.6 %spatial_attention.3 = (bf16[2,128,128]{2,1,0:T(8,128)(2,1)S(1)}, bf16[2,128,128]{2,1,0:T(8,128)(2,1)S(1)}, bf16[2,128,128]{2,1,0:T(8,128)(2,1)S(1)}, bf16[2,128,128]{2,1,0:T(8,128)(2,1)S(1)}) custom-call(s32[1]{0:T(128)} %bitcast.6.t_ref, s32[1]{0:T(128)} %bitcast.wide_ref.w_ref, bf16[6,3,128,128]{3,2,1,0:T(8,128)(2,1)} %copy-done.2, ...), custom_call_target="tpu_custom_call" | custom-call | bytes 32768 | tf_op jit(solution)/shard_map/cond/branch_0_fun/spatial_attention/pallas_call | solution.py:278
  67.5 1.2 collective-permute-start.5
  68.7 1.0 collective-permute-start.6
  70.4 1.9 %collective-permute-done.5.rest_0_ = bf16[2,128,128]{2,1,0:T(8,128)(2,1)S(1)} collective-permute-done((bf16[2,128,128]{2,1,0:T(8,128)(2,1)S(1)}, bf16[2,128,128]{2,1,0:T(8,128)(2,1)S(1)}, u32[]{:S(2)}, u32[]{:S(2)}) %collective-permute-start.5) | collective-permute-done | bytes 65568 | tf_op jit(solution)/shard_map/cond/branch_0_fun/ppermute | solution.py:343
  72.3 2.9 %collective-permute-done.6.rest_1_ = bf16[2,128,128]{2,1,0:T(8,128)(2,1)S(1)} collective-permute-done((bf16[2,128,128]{2,1,0:T(8,128)(2,1)S(1)}, bf16[2,128,128]{2,1,0:T(8,128)(2,1)S(1)}, u32[]{:S(2)}, u32[]{:S(2)}) %collective-permute-start.6) | collective-permute-done | bytes 65568 | tf_op jit(solution)/shard_map/cond/branch_0_fun/ppermute | solution.py:343
  75.6 4.1 %temporal_attention.2.refs_2_.refs_10_ = bf16[32,6,16,128]{3,2,1,0:T(8,128)(2,1)} custom-call(bf16[32,3,6,16,128]{4,3,2,1,0:T(8,128)(2,1)} %bitcast.5.in_ref, bf16[2,128,128]{2,1,0:T(8,128)(2,1)S(1)} %collective-permute-done.5.rest_0_, bf16[2,128,128]{2,1,0:T(8,128)(2,1)S(1)} %collective-permute-done.6.rest_1_, ...), custom_call_target="tpu_custom_call" | custom-call | bytes 196608 | tf_op jit(solution)/shard_map/cond/branch_0_fun/temporal_attention/pallas_call | solution.py:240
  79.7 11.0 %all-to-all-start.1 = ((bf16[32,96,128]{2,1,0:T(8,128)(2,1)}), bf16[32,96,128]{2,1,0:T(8,128)(2,1)S(1)}, u32[]{:S(2)}, u32[]{:S(2)}) async-start(bf16[32,96,128]{2,1,0:T(8,128)(2,1)} %bitcast.9), calls=%async_computation.1 | async-start | bytes 1572864 | tf_op jit(solution)/shard_map/cond/branch_0_fun/all_to_all | solution.py:390
  90.7 5.5 %collective-permute-done.8.refs_0_ = bf16[4,2,512,128]{3,2,1,0:T(8,128)(2,1)} collective-permute-done((bf16[4,2,512,128]{3,2,1,0:T(8,128)(2,1)}, bf16[4,2,512,128]{3,2,1,0:T(8,128)(2,1)}, u32[]{:S(2)}, u32[]{:S(2)}) %collective-permute-start.8) | collective-permute-done | bytes 1048608 | tf_op jit(solution)/shard_map/cond/branch_0_fun/ppermute | solution.py:354
  96.8 2.4 %collective-permute-done.10.refs_7_ = bf16[4,2,512,128]{3,2,1,0:T(8,128)(2,1)S(1)} collective-permute-done((bf16[4,2,512,128]{3,2,1,0:T(8,128)(2,1)}, bf16[4,2,512,128]{3,2,1,0:T(8,128)(2,1)S(1)}, u32[]{:S(2)}, u32[]{:S(2)}) %collective-permute-start.10) | collective-permute-done | bytes 1048608 | tf_op jit(solution)/shard_map/cond/branch_0_fun/ppermute | solution.py:348
  99.1 1.5 %collective-permute-done.11.refs_9_ = bf16[4,2,512,128]{3,2,1,0:T(8,128)(2,1)S(1)} collective-permute-done((bf16[4,2,512,128]{3,2,1,0:T(8,128)(2,1)}, bf16[4,2,512,128]{3,2,1,0:T(8,128)(2,1)S(1)}, u32[]{:S(2)}, u32[]{:S(2)}) %collective-permute-start.11) | collective-permute-done | bytes 1048608 | tf_op jit(solution)/shard_map/cond/branch_0_fun/ppermute | solution.py:348
  100.6 10.2 %spatial_attention.4 = (bf16[4,128,128]{2,1,0:T(8,128)(2,1)S(1)}, bf16[4,128,128]{2,1,0:T(8,128)(2,1)S(1)}, bf16[4,128,128]{2,1,0:T(8,128)(2,1)S(1)}, bf16[4,128,128]{2,1,0:T(8,128)(2,1)S(1)}) custom-call(s32[1]{0:T(128)} %bitcast.6.t_ref, s32[1]{0:T(128)} %bitcast.wide_ref.w_ref, bf16[6,3,128,128]{3,2,1,0:T(8,128)(2,1)} %copy-done.2, ...), custom_call_target="tpu_custom_call" | custom-call | bytes 65536 | tf_op jit(solution)/shard_map/cond/branch_0_fun/spatial_attention/pallas_call | solution.py:278
  111.5 5.6 %collective-permute-start.12 = (bf16[4,128,128]{2,1,0:T(8,128)(2,1)S(1)}, bf16[4,128,128]{2,1,0:T(8,128)(2,1)S(1)}, u32[]{:S(2)}, u32[]{:S(2)}) collective-permute-start(bf16[4,128,128]{2,1,0:T(8,128)(2,1)S(1)} %get-tuple-element.53), channel_id=1, source_target_pairs={{0,6},{1,7},{2,0},{3,1},{4,2},{5,3},{6,4},{7,5},{8,14},{9,15},{10,... | collective-permute-start | bytes 393224 | tf_op jit(solution)/shard_map/cond/branch_0_fun/ppermute | solution.py:343
  117.1 1.5 %collective-permute-start.13 = (bf16[4,128,128]{2,1,0:T(8,128)(2,1)S(1)}, bf16[4,128,128]{2,1,0:T(8,128)(2,1)S(1)}, u32[]{:S(2)}, u32[]{:S(2)}) collective-permute-start(bf16[4,128,128]{2,1,0:T(8,128)(2,1)S(1)} %get-tuple-element.54), channel_id=1, source_target_pairs={{0,4},{1,5},{2,6},{3,7},{4,0},{5,1},{6,2},{7,3},{8,12},{9,13},{10,... | collective-permute-start | bytes 393224 | tf_op jit(solution)/shard_map/cond/branch_0_fun/ppermute | solution.py:343
  118.6 1.4 %collective-permute-start.14 = (bf16[4,128,128]{2,1,0:T(8,128)(2,1)S(1)}, bf16[4,128,128]{2,1,0:T(8,128)(2,1)S(1)}, u32[]{:S(2)}, u32[]{:S(2)}) collective-permute-start(bf16[4,128,128]{2,1,0:T(8,128)(2,1)S(1)} %get-tuple-element.55), channel_id=1, source_target_pairs={{0,2},{1,3},{2,4},{3,5},{4,6},{5,7},{6,0},{7,1},{8,10},{9,11},{10,... | collective-permute-start | bytes 393224 | tf_op jit(solution)/shard_map/cond/branch_0_fun/ppermute | solution.py:343
  120.0 3.0 %collective-permute-done.12 = bf16[4,128,128]{2,1,0:T(8,128)(2,1)S(1)} collective-permute-done((bf16[4,128,128]{2,1,0:T(8,128)(2,1)S(1)}, bf16[4,128,128]{2,1,0:T(8,128)(2,1)S(1)}, u32[]{:S(2)}, u32[]{:S(2)}) %collective-permute-start.12) | collective-permute-done | bytes 131104 | tf_op jit(solution)/shard_map/cond/branch_0_fun/ppermute | solution.py:343
  123.0 2.0 %collective-permute-done.13 = bf16[4,128,128]{2,1,0:T(8,128)(2,1)S(1)} collective-permute-done((bf16[4,128,128]{2,1,0:T(8,128)(2,1)S(1)}, bf16[4,128,128]{2,1,0:T(8,128)(2,1)S(1)}, u32[]{:S(2)}, u32[]{:S(2)}) %collective-permute-start.13) | collective-permute-done | bytes 131104 | tf_op jit(solution)/shard_map/cond/branch_0_fun/ppermute | solution.py:343
  125.0 1.7 %collective-permute-done.14 = bf16[4,128,128]{2,1,0:T(8,128)(2,1)S(1)} collective-permute-done((bf16[4,128,128]{2,1,0:T(8,128)(2,1)S(1)}, bf16[4,128,128]{2,1,0:T(8,128)(2,1)S(1)}, u32[]{:S(2)}, u32[]{:S(2)}) %collective-permute-start.14) | collective-permute-done | bytes 131104 | tf_op jit(solution)/shard_map/cond/branch_0_fun/ppermute | solution.py:343
  127.3 4.1 %unpack.2 = bf16[8,16,5120]{2,1,0:T(8,128)(2,1)} custom-call(s32[40]{0:T(128)S(1)} %copy-done.31, s32[40]{0:T(128)S(1)} %copy-done.29, s32[1]{0:T(128)} %bitcast.wide_ref.w_ref, bf16[32,6,16,128]{3,2,1,0:T(8,128)(2,1)S(1)} %bitcast.40, bf16[4,8,16,128]{3,2,1,0:T(8,128)(2,1)} %bitcast.47, bf16[4,8,16,128]{3,2,1,0:T(8,128)(2,1)} %bitcast.60, ...), custom_call_target="tpu_custom_call" | custom-call | bytes 2621440 | tf_op jit(solution)/shard_map/cond/branch_0_fun/unpack/pallas_call | solution.py:328
  (51 shorter events, 4.8 us)
Async XLA Ops:
  7.5 11.4 %copy-start.18 = (bf16[128,5120]{1,0:T(8,128)(2,1)S(1)}, bf16[128,5120]{1,0:T(8,128)(2,1)}, u32[]{:S(2)}) copy-start(bf16[128,5120]{1,0:T(8,128)(2,1)} %get-tuple-element.85.q_ref) | copy-start | bytes 3932164 | tf_op jit(solution)/shard_map/cond
  7.5 11.4 %copy-start.20 = (bf16[128,5120]{1,0:T(8,128)(2,1)S(1)}, bf16[128,5120]{1,0:T(8,128)(2,1)}, u32[]{:S(2)}) copy-start(bf16[128,5120]{1,0:T(8,128)(2,1)} %get-tuple-element.87.k_ref) | copy-start | bytes 3932164 | tf_op jit(solution)/shard_map/cond
  7.5 11.4 %copy-start.29 = (s32[40]{0:T(128)S(1)}, s32[40]{0:T(128)}, u32[]{:S(2)}) copy-start(s32[40]{0:T(128)} %get-tuple-element.37.win_ref) | copy-start | bytes 484 | tf_op jit(solution)/shard_map/cond
  7.5 11.4 %copy-start.31 = (s32[40]{0:T(128)S(1)}, s32[40]{0:T(128)}, u32[]{:S(2)}) copy-start(s32[40]{0:T(128)} %get-tuple-element.36.kind_ref) | copy-start | bytes 484 | tf_op jit(solution)/shard_map/cond
  7.5 68.0 %all-to-all-start = ((bf16[32,288,128]{2,1,0:T(8,128)(2,1)}), bf16[32,288,128]{2,1,0:T(8,128)(2,1)}, u32[]{:S(2)}, u32[]{:S(2)}) async-start(bf16[32,288,128]{2,1,0:T(8,128)(2,1)} %bitcast.4), calls=%async_computation | async-start | bytes 4718592 | tf_op jit(solution)/shard_map/cond/branch_0_fun/all_to_all | solution.py:366
  22.4 37.0 %copy-start.2 = (bf16[6,3,128,128]{3,2,1,0:T(8,128)(2,1)}, bf16[6,3,128,128]{3,2,1,0:T(8,128)(2,1)S(1)}, u32[]{:S(2)}) copy-start(bf16[6,3,128,128]{3,2,1,0:T(8,128)(2,1)S(1)} %get-tuple-element.43.refs_0_) | copy-start | bytes 1769476 | tf_op jit(solution)/shard_map/cond
  22.4 16.4 %collective-permute-start = (bf16[6,3,128,128]{3,2,1,0:T(8,128)(2,1)S(1)}, bf16[6,3,128,128]{3,2,1,0:T(8,128)(2,1)S(1)}, u32[]{:S(2)}, u32[]{:S(2)}) collective-permute-start(bf16[6,3,128,128]{3,2,1,0:T(8,128)(2,1)S(1)} %get-tuple-element.44), channel_id=1, source_target_pairs={{0,2},{1,3},{2,4},{3,5},{4,6},{5,7},{6,0},{7,1},{8,10},{9,11},{10,... | collective-permute-start | bytes 1769480 | tf_op jit(solution)/shard_map/cond/branch_0_fun/ppermute | solution.py:343
  24.1 28.0 %collective-permute-start.1 = (bf16[6,3,128,128]{3,2,1,0:T(8,128)(2,1)S(1)}, bf16[6,3,128,128]{3,2,1,0:T(8,128)(2,1)S(1)}, u32[]{:S(2)}, u32[]{:S(2)}) collective-permute-start(bf16[6,3,128,128]{3,2,1,0:T(8,128)(2,1)S(1)} %get-tuple-element.45), channel_id=1, source_target_pairs={{0,4},{1,5},{2,6},{3,7},{4,0},{5,1},{6,2},{7,3},{8,12},{9,13},{10,... | collective-permute-start | bytes 1769480 | tf_op jit(solution)/shard_map/cond/branch_0_fun/ppermute | solution.py:343
  26.9 25.1 %collective-permute-start.2 = (bf16[6,3,128,128]{3,2,1,0:T(8,128)(2,1)S(1)}, bf16[6,3,128,128]{3,2,1,0:T(8,128)(2,1)S(1)}, u32[]{:S(2)}, u32[]{:S(2)}) collective-permute-start(bf16[6,3,128,128]{3,2,1,0:T(8,128)(2,1)S(1)} %get-tuple-element.46), channel_id=1, source_target_pairs={{0,6},{1,7},{2,0},{3,1},{4,2},{5,3},{6,4},{7,5},{8,14},{9,15},{10,... | collective-permute-start | bytes 1769480 | tf_op jit(solution)/shard_map/cond/branch_0_fun/ppermute | solution.py:343
  38.8 20.6 %copy-start.3 = (bf16[6,3,128,128]{3,2,1,0:T(8,128)(2,1)}, bf16[6,3,128,128]{3,2,1,0:T(8,128)(2,1)S(1)}, u32[]{:S(2)}) copy-start(bf16[6,3,128,128]{3,2,1,0:T(8,128)(2,1)S(1)} %collective-permute-done.refs_1_) | copy-start | bytes 1769476 | tf_op jit(solution)/shard_map/cond
  52.1 7.4 %copy-start.4 = (bf16[6,3,128,128]{3,2,1,0:T(8,128)(2,1)}, bf16[6,3,128,128]{3,2,1,0:T(8,128)(2,1)S(1)}, u32[]{:S(2)}) copy-start(bf16[6,3,128,128]{3,2,1,0:T(8,128)(2,1)S(1)} %collective-permute-done.1.refs_2_) | copy-start | bytes 1769476 | tf_op jit(solution)/shard_map/cond
  52.1 7.4 %copy-start.5 = (bf16[6,3,128,128]{3,2,1,0:T(8,128)(2,1)}, bf16[6,3,128,128]{3,2,1,0:T(8,128)(2,1)S(1)}, u32[]{:S(2)}) copy-start(bf16[6,3,128,128]{3,2,1,0:T(8,128)(2,1)S(1)} %collective-permute-done.2.refs_3_) | copy-start | bytes 1769476 | tf_op jit(solution)/shard_map/cond
  53.2 8.2 %collective-permute-start.4 = (bf16[4,2,512,128]{3,2,1,0:T(8,128)(2,1)}, bf16[4,2,512,128]{3,2,1,0:T(8,128)(2,1)S(1)}, u32[]{:S(2)}, u32[]{:S(2)}) collective-permute-start(bf16[4,2,512,128]{3,2,1,0:T(8,128)(2,1)} %bitcast.8.refs_4_), channel_id=1, source_target_pairs={{0,1},{1,0},{2,3},{3,2},{4,5},{5,4},{6,7},{7,6},{8,9},{9,8},{10,11... | collective-permute-start | bytes 3145736 | tf_op jit(solution)/shard_map/cond/branch_0_fun/ppermute | solution.py:348
  53.3 42.8 %collective-permute-start.8 = (bf16[4,2,512,128]{3,2,1,0:T(8,128)(2,1)}, bf16[4,2,512,128]{3,2,1,0:T(8,128)(2,1)}, u32[]{:S(2)}, u32[]{:S(2)}) collective-permute-start(bf16[4,2,512,128]{3,2,1,0:T(8,128)(2,1)} %bitcast.8.refs_4_), channel_id=1, source_target_pairs={{0,8},{8,16},{16,24},{24,32},{32,40},{40,48},{48,56},{56,64},{64,7... | collective-permute-start | bytes 3145736 | tf_op jit(solution)/shard_map/cond/branch_0_fun/ppermute | solution.py:354
  56.7 39.4 %collective-permute-start.9 = (bf16[4,2,512,128]{3,2,1,0:T(8,128)(2,1)}, bf16[4,2,512,128]{3,2,1,0:T(8,128)(2,1)}, u32[]{:S(2)}, u32[]{:S(2)}) collective-permute-start(bf16[4,2,512,128]{3,2,1,0:T(8,128)(2,1)} %bitcast.8.refs_4_), channel_id=1, source_target_pairs={{8,0},{16,8},{24,16},{32,24},{40,32},{48,40},{56,48},{64,56},{72,6... | collective-permute-start | bytes 3145736 | tf_op jit(solution)/shard_map/cond/branch_0_fun/ppermute | solution.py:354
  59.5 2.0 %copy-start.11 = (bf16[2,2,4,128,128]{4,3,2,1,0:T(8,128)(2,1)}, bf16[2,2,4,128,128]{4,3,2,1,0:T(8,128)(2,1)S(1)}, u32[]{:S(2)}) copy-start(bf16[2,2,4,128,128]{4,3,2,1,0:T(8,128)(2,1)S(1)} %assemble.3) | copy-start | bytes 1572868 | tf_op jit(solution)/shard_map/cond
  59.5 2.0 %collective-permute-start.3 = (bf16[2,2,512,128]{3,2,1,0:T(8,128)(2,1)S(1)}, bf16[2,2,512,128]{3,2,1,0:T(8,128)(2,1)S(1)}, u32[]{:S(2)}, u32[]{:S(2)}) collective-permute-start(bf16[2,2,512,128]{3,2,1,0:T(8,128)(2,1)S(1)} %bitcast.41), channel_id=1, source_target_pairs={{0,1},{1,0},{2,3},{3,2},{4,5},{5,4},{6,7},{7,6},{8,9},{9,8},{10,11... | collective-permute-start | bytes 1572872 | tf_op jit(solution)/shard_map/cond/branch_0_fun/ppermute | solution.py:348
  61.5 18.2 %copy-start.6 = (bf16[4,2,512,128]{3,2,1,0:T(8,128)(2,1)}, bf16[4,2,512,128]{3,2,1,0:T(8,128)(2,1)S(1)}, u32[]{:S(2)}) copy-start(bf16[4,2,512,128]{3,2,1,0:T(8,128)(2,1)S(1)} %collective-permute-done.4.refs_6_.refs_5_) | copy-start | bytes 3145732 | tf_op jit(solution)/shard_map/cond
  67.5 4.8 %collective-permute-start.5 = (bf16[2,128,128]{2,1,0:T(8,128)(2,1)S(1)}, bf16[2,128,128]{2,1,0:T(8,128)(2,1)S(1)}, u32[]{:S(2)}, u32[]{:S(2)}) collective-permute-start(bf16[2,128,128]{2,1,0:T(8,128)(2,1)S(1)} %get-tuple-element.47), channel_id=1, source_target_pairs={{0,6},{1,7},{2,0},{3,1},{4,2},{5,3},{6,4},{7,5},{8,14},{9,15},{10,... | collective-permute-start | bytes 196616 | tf_op jit(solution)/shard_map/cond/branch_0_fun/ppermute | solution.py:343
  68.7 6.5 %collective-permute-start.6 = (bf16[2,128,128]{2,1,0:T(8,128)(2,1)S(1)}, bf16[2,128,128]{2,1,0:T(8,128)(2,1)S(1)}, u32[]{:S(2)}, u32[]{:S(2)}) collective-permute-start(bf16[2,128,128]{2,1,0:T(8,128)(2,1)S(1)} %get-tuple-element.48), channel_id=1, source_target_pairs={{0,4},{1,5},{2,6},{3,7},{4,0},{5,1},{6,2},{7,3},{8,12},{9,13},{10,... | collective-permute-start | bytes 196616 | tf_op jit(solution)/shard_map/cond/branch_0_fun/ppermute | solution.py:343
  69.7 5.8 %collective-permute-start.7 = (bf16[2,128,128]{2,1,0:T(8,128)(2,1)S(1)}, bf16[2,128,128]{2,1,0:T(8,128)(2,1)S(1)}, u32[]{:S(2)}, u32[]{:S(2)}) collective-permute-start(bf16[2,128,128]{2,1,0:T(8,128)(2,1)S(1)} %get-tuple-element.49), channel_id=1, source_target_pairs={{0,2},{1,3},{2,4},{3,5},{4,6},{5,7},{6,0},{7,1},{8,10},{9,11},{10,... | collective-permute-start | bytes 196616 | tf_op jit(solution)/shard_map/cond/branch_0_fun/ppermute | solution.py:343
  72.3 23.8 %copy-start.13 = (bf16[2,128,128]{2,1,0:T(8,128)(2,1)}, bf16[2,128,128]{2,1,0:T(8,128)(2,1)S(1)}, u32[]{:S(2)}) copy-start(bf16[2,128,128]{2,1,0:T(8,128)(2,1)S(1)} %collective-permute-done.5.rest_0_) | copy-start | bytes 196612 | tf_op jit(solution)/shard_map/cond
  75.2 21.0 %copy-start.14 = (bf16[2,128,128]{2,1,0:T(8,128)(2,1)}, bf16[2,128,128]{2,1,0:T(8,128)(2,1)S(1)}, u32[]{:S(2)}) copy-start(bf16[2,128,128]{2,1,0:T(8,128)(2,1)S(1)} %collective-permute-done.6.rest_1_) | copy-start | bytes 196612 | tf_op jit(solution)/shard_map/cond
  75.6 20.6 %copy-start.15 = (bf16[2,128,128]{2,1,0:T(8,128)(2,1)}, bf16[2,128,128]{2,1,0:T(8,128)(2,1)S(1)}, u32[]{:S(2)}) copy-start(bf16[2,128,128]{2,1,0:T(8,128)(2,1)S(1)} %collective-permute-done.7.rest_2_) | copy-start | bytes 196612 | tf_op jit(solution)/shard_map/cond
  79.7 47.0 %all-to-all-start.1 = ((bf16[32,96,128]{2,1,0:T(8,128)(2,1)}), bf16[32,96,128]{2,1,0:T(8,128)(2,1)S(1)}, u32[]{:S(2)}, u32[]{:S(2)}) async-start(bf16[32,96,128]{2,1,0:T(8,128)(2,1)} %bitcast.9), calls=%async_computation.1 | async-start | bytes 1572864 | tf_op jit(solution)/shard_map/cond/branch_0_fun/all_to_all | solution.py:390
  96.2 3.0 %collective-permute-start.10 = (bf16[4,2,512,128]{3,2,1,0:T(8,128)(2,1)}, bf16[4,2,512,128]{3,2,1,0:T(8,128)(2,1)S(1)}, u32[]{:S(2)}, u32[]{:S(2)}) collective-permute-start(bf16[4,2,512,128]{3,2,1,0:T(8,128)(2,1)} %get-tuple-element.50.refs_6_), channel_id=1, source_target_pairs={{0,1},{1,0},{2,3},{3,2},{4,5},{5,4},{6,7},{7,6},{8,9},{9,8},{10,11... | collective-permute-start | bytes 3145736 | tf_op jit(solution)/shard_map/cond/branch_0_fun/ppermute | solution.py:348
  96.3 4.4 %collective-permute-start.11 = (bf16[4,2,512,128]{3,2,1,0:T(8,128)(2,1)}, bf16[4,2,512,128]{3,2,1,0:T(8,128)(2,1)S(1)}, u32[]{:S(2)}, u32[]{:S(2)}) collective-permute-start(bf16[4,2,512,128]{3,2,1,0:T(8,128)(2,1)} %get-tuple-element.51.refs_8_), channel_id=1, source_target_pairs={{0,1},{1,0},{2,3},{3,2},{4,5},{5,4},{6,7},{7,6},{8,9},{9,8},{10,11... | collective-permute-start | bytes 3145736 | tf_op jit(solution)/shard_map/cond/branch_0_fun/ppermute | solution.py:348
  111.5 11.5 %collective-permute-start.12 = (bf16[4,128,128]{2,1,0:T(8,128)(2,1)S(1)}, bf16[4,128,128]{2,1,0:T(8,128)(2,1)S(1)}, u32[]{:S(2)}, u32[]{:S(2)}) collective-permute-start(bf16[4,128,128]{2,1,0:T(8,128)(2,1)S(1)} %get-tuple-element.53), channel_id=1, source_target_pairs={{0,6},{1,7},{2,0},{3,1},{4,2},{5,3},{6,4},{7,5},{8,14},{9,15},{10,... | collective-permute-start | bytes 393224 | tf_op jit(solution)/shard_map/cond/branch_0_fun/ppermute | solution.py:343
  117.1 7.9 %collective-permute-start.13 = (bf16[4,128,128]{2,1,0:T(8,128)(2,1)S(1)}, bf16[4,128,128]{2,1,0:T(8,128)(2,1)S(1)}, u32[]{:S(2)}, u32[]{:S(2)}) collective-permute-start(bf16[4,128,128]{2,1,0:T(8,128)(2,1)S(1)} %get-tuple-element.54), channel_id=1, source_target_pairs={{0,4},{1,5},{2,6},{3,7},{4,0},{5,1},{6,2},{7,3},{8,12},{9,13},{10,... | collective-permute-start | bytes 393224 | tf_op jit(solution)/shard_map/cond/branch_0_fun/ppermute | solution.py:343
  118.6 8.1 %collective-permute-start.14 = (bf16[4,128,128]{2,1,0:T(8,128)(2,1)S(1)}, bf16[4,128,128]{2,1,0:T(8,128)(2,1)S(1)}, u32[]{:S(2)}, u32[]{:S(2)}) collective-permute-start(bf16[4,128,128]{2,1,0:T(8,128)(2,1)S(1)} %get-tuple-element.55), channel_id=1, source_target_pairs={{0,2},{1,3},{2,4},{3,5},{4,6},{5,7},{6,0},{7,1},{8,10},{9,11},{10,... | collective-permute-start | bytes 393224 | tf_op jit(solution)/shard_map/cond/branch_0_fun/ppermute | solution.py:343
  123.0 3.7 %copy-start.26 = (bf16[4,128,128]{2,1,0:T(8,128)(2,1)}, bf16[4,128,128]{2,1,0:T(8,128)(2,1)S(1)}, u32[]{:S(2)}) copy-start(bf16[4,128,128]{2,1,0:T(8,128)(2,1)S(1)} %collective-permute-done.12) | copy-start | bytes 393220 | tf_op jit(solution)/shard_map/cond
  125.0 1.7 %copy-start.27 = (bf16[4,128,128]{2,1,0:T(8,128)(2,1)}, bf16[4,128,128]{2,1,0:T(8,128)(2,1)S(1)}, u32[]{:S(2)}) copy-start(bf16[4,128,128]{2,1,0:T(8,128)(2,1)S(1)} %collective-permute-done.13) | copy-start | bytes 393220 | tf_op jit(solution)/shard_map/cond
  (4 other events, 2.7 us)
